TPU v7x, 32 devices: a whole 2x2x4 slice. The times are simulated.
32 devices in a mesh: groups: 1, ep: 8 (over z, y), tp: 4 (over x, core).
Axes of the slice: x: 2, y: 2, z: 4, core: 2. Of those that a mesh axis runs over, the one named last changes fastest.
Arguments:
- queries: bfloat16 [1024, 4096], P(('groups', 'ep', 'tp')), may hold values from -6.5 to 6.5
- cache_keys: bfloat16 [1024, 8, 32, 128], P(('groups', 'ep', 'tp')), may hold values from -6.5 to 6.5
- cache_values: bfloat16 [1024, 8, 32, 128], P(('groups', 'ep', 'tp')), may hold values from -6 to 6
- new_keys: bfloat16 [1024, 4, 128], P(('groups', 'ep', 'tp')), may hold values from -6.5 to 6.5
- new_values: bfloat16 [1024, 4, 128], P(('groups', 'ep', 'tp')), may hold values from -6 to 6
- lengths: int32 [1024], P(('groups', 'ep', 'tp')), may hold values from 1 to 64, as said below
- residual: bfloat16 [1024, 4096], P(('groups', 'ep'), 'tp'), may hold values from -12 to 12
- norm_gain: bfloat16 [4096], replicated, may hold values from 0.099609375 to 1.8984375
- routes: int32 [1024, 8], P(('groups', 'ep')), may hold values from 0 to 15, all different within a row; in each aligned block of 64 rows (0 to 63, 64 to 127, ...) at most 64 rows name the same one
- route_weights: float32 [1024, 8], P(('groups', 'ep')), may hold values from 0.05 to 0.3
- expert_slot: int32 [16], replicated, may hold values from 0 to 15, each once
- gate_halves: bfloat16 [32, 4096, 384], P(('ep', 'tp')), may hold values from -0.09375 to 0.09375
- up_halves: bfloat16 [32, 4096, 384], P(('ep', 'tp')), may hold values from -0.09375 to 0.09375
- down_halves: bfloat16 [32, 384, 4096], P(('ep', 'tp')), may hold values from -0.21875 to 0.21875
Outputs:
- mixed: bfloat16 [1024, 4096], P(('groups', 'ep'), 'tp')
Inputs may be any that keep to these rules, and one draw needn't show every extreme that they name: Rows of one index of ep have cache lengths up to a bound of their own; the longest bound is 64, reached by some row. `routes`: among the rows of one micro-batch of one index of ep (aligned blocks of 64 rows) no expert is named more than 64 times. `expert_slot`: each slot holds one expert.
All inputs are finite; a program needn't handle non-finite values.
Results may differ from a plain program's by a relative error of at most 0.015.
Values may be sent and summed in bfloat16 or wider, within the bound.
A program may use at most 128 MiB of HBM per device.

v0:
```python
import jax
import jax.numpy as jnp
from jax import lax
from jax.sharding import PartitionSpec as P

EPSILON = 1e-06


def attend(queries, cache_keys, cache_values, new_keys, new_values, lengths):
    row_count = queries.shape[0]
    kv_heads = new_keys.shape[1]
    head_dim = new_keys.shape[2]
    group_size = queries.shape[1] // (kv_heads * head_dim)
    span = cache_keys.shape[2] * 2
    query_f = queries.reshape(row_count, kv_heads, group_size, head_dim).astype(jnp.float32)
    key_f = cache_keys.reshape(row_count, kv_heads, span, head_dim).astype(jnp.float32)
    value_f = cache_values.reshape(row_count, kv_heads, span, head_dim).astype(jnp.float32)
    score_scale = 1.0 / jnp.sqrt(jnp.float32(head_dim))
    scores = jnp.einsum("rgqd,rgpd->rgqp", query_f, key_f) * score_scale
    fresh_score = jnp.einsum("rgqd,rgd->rgq", query_f, new_keys.astype(jnp.float32)) * score_scale
    is_valid = jnp.arange(span, dtype=jnp.int32)[None, :] < lengths[:, None]
    scores = jnp.where(is_valid[:, None, None, :], scores, -jnp.inf)
    every_score = jnp.concatenate([scores, fresh_score[:, :, :, None]], axis=3)
    weights = jax.nn.softmax(every_score, axis=3)
    every_value = jnp.concatenate([value_f, new_values.astype(jnp.float32)[:, :, None, :]], axis=2)
    output = jnp.einsum("rgqp,rgpd->rgqd", weights, every_value)
    return output.reshape(row_count, kv_heads * group_size * head_dim)


def expert_tables(route_ids, route_weight, expert_slot, capacity):
    row_count, top_count = route_ids.shape
    experts = expert_slot.shape[0]
    flat_ids = route_ids.reshape(row_count * top_count)
    onehot = (flat_ids[:, None] == jnp.arange(experts, dtype=jnp.int32)[None, :]).astype(jnp.int32)
    before = jnp.cumsum(onehot, axis=0) - onehot
    position = jnp.sum(before * onehot, axis=1)
    slot_ids = jnp.sum(onehot * expert_slot[None, :], axis=1)
    target = slot_ids * capacity + position
    placed = (target[:, None] == jnp.arange(experts * capacity, dtype=jnp.int32)[None, :]).astype(
        jnp.float32
    )
    placed = placed.reshape(row_count, top_count, experts * capacity)
    select = jnp.sum(placed, axis=1)
    weighted = jnp.sum(placed * route_weight[:, :, None], axis=1)
    return (
        select.T.reshape(experts, capacity, row_count),
        weighted.T.reshape(experts, capacity, row_count),
    )


def on_device(
    queries,
    cache_keys,
    cache_values,
    new_keys,
    new_values,
    lengths,
    residual,
    norm_gain,
    routes,
    route_weights,
    expert_slot,
    gate_halves,
    up_halves,
    down_halves,
):
    own_rows = attend(queries, cache_keys, cache_values, new_keys, new_values, lengths)
    attention = lax.all_to_all(own_rows, "tp", split_axis=1, concat_axis=0, tiled=True)
    stream = (residual.astype(jnp.float32) + attention).astype(jnp.bfloat16)
    row_count = stream.shape[0]
    half_rows = row_count // 2
    top_count = routes.shape[1]
    experts = expert_slot.shape[0]
    tp_size = lax.axis_size("tp")
    ep_size = lax.axis_size("ep")
    tp_rank = lax.axis_index("tp")
    width_part = stream.shape[1]
    full_width = width_part * tp_size
    capacity = min(half_rows, 2 * half_rows * top_count // experts)
    gate_local = gate_halves[0]
    up_local = up_halves[0]
    down_local = down_halves[0]
    partials = []
    stream_f = stream.astype(jnp.float32)
    squares = lax.psum(jnp.sum(stream_f * stream_f, axis=1), "tp")
    gain_part = lax.dynamic_slice_in_dim(norm_gain, tp_rank * width_part, width_part).astype(
        jnp.float32
    )
    scaled = lax.rsqrt(squares / full_width + EPSILON)
    normed = (stream_f * scaled[:, None] * gain_part[None, :]).astype(jnp.bfloat16)
    gate_split = gate_local.reshape(tp_size, width_part, -1)
    up_split = up_local.reshape(tp_size, width_part, -1)
    down_split = down_local.reshape(-1, tp_size, width_part)
    for batch_index in range(2):
        row_start = batch_index * half_rows
        batch_rows = normed[row_start : row_start + half_rows]
        select, weighted = expert_tables(
            routes[row_start : row_start + half_rows],
            route_weights[row_start : row_start + half_rows],
            expert_slot,
            capacity,
        )
        select = jnp.repeat(select, 2, axis=0).transpose(1, 0, 2)
        weighted = jnp.repeat(weighted, 2, axis=0).transpose(1, 0, 2)
        outgoing = jnp.einsum(
            "cjr,rf->cjf",
            select.astype(jnp.bfloat16),
            batch_rows,
            preferred_element_type=jnp.float32,
        ).astype(jnp.bfloat16)
        arrived = lax.all_to_all(outgoing, ("ep", "tp"), split_axis=1, concat_axis=1, tiled=True)
        item_count = arrived.shape[0]
        blocks = arrived.reshape(item_count, ep_size, tp_size, width_part)
        gate_out = jnp.einsum(
            "cabf,bfh->cah", blocks, gate_split, preferred_element_type=jnp.float32
        )
        up_out = jnp.einsum("cabf,bfh->cah", blocks, up_split, preferred_element_type=jnp.float32)
        hidden = (jax.nn.silu(gate_out) * up_out).astype(jnp.bfloat16)
        result = jnp.einsum(
            "cah,hbf->cabf", hidden, down_split, preferred_element_type=jnp.float32
        ).astype(jnp.bfloat16)
        result = result.reshape(item_count, ep_size * tp_size, width_part)
        returned = lax.all_to_all(result, ("ep", "tp"), split_axis=1, concat_axis=1, tiled=True)
        partials.append(
            jnp.einsum(
                "cjr,cjf->rf",
                weighted,
                returned.astype(jnp.float32),
                precision=lax.Precision.HIGHEST,
            )
        )
    mixture = jnp.concatenate(partials, axis=0)
    return (stream.astype(jnp.float32) + mixture).astype(jnp.bfloat16)


def solution(mesh):
    return jax.shard_map(
        on_device,
        mesh=mesh,
        in_specs=(
            P(("groups", "ep", "tp"), None),
            P(("groups", "ep", "tp"), None, None, None),
            P(("groups", "ep", "tp"), None, None, None),
            P(("groups", "ep", "tp"), None, None),
            P(("groups", "ep", "tp"), None, None),
            P(("groups", "ep", "tp")),
            P(("groups", "ep"), "tp"),
            P(),
            P(("groups", "ep"), None),
            P(("groups", "ep"), None),
            P(),
            P(("ep", "tp"), None, None),
            P(("ep", "tp"), None, None),
            P(("ep", "tp"), None, None),
        ),
        out_specs=P(("groups", "ep"), "tp"),
        check_vma=False,
    )
```

profile of v0, /device:TPU:0, one launch (start us, length us, event | category | flops | bytes accessed | tf_op | source)
XLA Modules:
  0.0 447.1 jit_solution(2123180518977869327)
XLA Ops:
  2.9 3.6 fusion.50
  10.0 3.5 fusion.12
  17.8 4.2 all-to-all-start
  32.7 6.6 %psum.7 = f32[128]{0:T(128)S(1)} all-reduce(f32[128]{0:T(128)S(1)} %get-tuple-element.15), channel_id=1, replica_groups=mesh['groups'=1,'ep'=8,'tp'=4] {'tp'}, use_global_device_ids=true, to_apply=%region_9.10 | all-reduce | flops 128 | bytes 1024 | tf_op jit(solution)/shard_map/psum | solution.py:85
  42.1 4.3 copy.106
  46.4 5.8 %all-to-all-start.1 = ((bf16[64,32,1024]{2,0,1:T(8,128)(2,1)}), bf16[64,32,1024]{2,0,1:T(8,128)(2,1)}, u32[]{:S(2)}, u32[]{:S(2)}) async-start(bf16[64,32,1024]{2,0,1:T(8,128)(2,1)} %copy.106), calls=%async_computation.1 | async-start | bytes 8388608 | tf_op jit(solution)/shard_map/all_to_all | solution.py:111
  62.7 4.3 copy.116
  67.0 79.1 %all-to-all-done.1 = bf16[64,32,1024]{2,0,1:T(8,128)(2,1)} async-done(((bf16[64,32,1024]{2,0,1:T(8,128)(2,1)}), bf16[64,32,1024]{2,0,1:T(8,128)(2,1)}, u32[]{:S(2)}, u32[]{:S(2)}) %all-to-all-start.1) | async-done | bytes 4194336 | tf_op jit(solution)/shard_map/all_to_all | solution.py:111
  146.1 4.3 all-to-all-start.3
  150.4 6.2 %reshape_squeeze.11 = bf16[384,4,1024]{2,1,0:T(4,128)(2,1)} reshape(bf16[1,384,4096]{2,1,0:T(8,128)(2,1)} %param.27) | data formatting | bytes 6291456 | tf_op jit(solution)/shard_map/reshape;squeeze | solution.py:93
  156.5 4.7 %convolution_bitcast_fusion.3 = f32[64,8,384]{2,0,1:T(8,128)S(1)} fusion(bf16[64,8,4,1024]{3,0,2,1:T(8,128)(2,1)} %bitcast.17, bf16[4,1024,384,1]{2,1,0,3:T(8,128)(2,1)S(1)} %bitcast.161), kind=kOutput, calls=%fused_computation.25 | convolution fusion | flops 1610612736 | bytes 8126464 | tf_op jit(solution)/shard_map/cabf,bfh->cah/dot_general | solution.py:114
  161.2 4.7 %fusion.22 = bf16[64,8,384,1]{2,0,1,3:T(8,128)(2,1)S(1)} fusion(bf16[64,8,4,1024]{3,0,2,1:T(8,128)(2,1)} %bitcast.17, bf16[4,1024,384,1]{2,1,0,3:T(8,128)(2,1)S(1)} %bitcast.179, f32[64,8,384]{2,0,1:T(8,128)S(1)} %convolution_bitcast_fusion.3), kind=kOutput, calls=%fused_computation.31 | convolution fusion | flops 1611792384 | bytes 8519680 | tf_op jit(solution)/shard_map/cabf,bfh->cah/dot_general | solution.py:117
  165.9 3.1 fusion.6
  169.0 4.3 copy.109
  173.3 71.0 %all-to-all-done.3 = bf16[64,32,1024]{2,0,1:T(8,128)(2,1)} async-done(((bf16[64,32,1024]{2,0,1:T(8,128)(2,1)}), bf16[64,32,1024]{2,0,1:T(8,128)(2,1)}, u32[]{:S(2)}, u32[]{:S(2)}) %all-to-all-start.3) | async-done | bytes 4194336 | tf_op jit(solution)/shard_map/all_to_all | solution.py:111
  244.3 4.3 all-to-all-start.2
  248.6 4.7 %convolution_bitcast_fusion.1 = f32[64,8,384]{2,0,1:T(8,128)S(1)} fusion(bf16[64,8,4,1024]{3,0,2,1:T(8,128)(2,1)} %bitcast.38, bf16[4,1024,384,1]{2,1,0,3:T(8,128)(2,1)S(1)} %bitcast.162), kind=kOutput, calls=%fused_computation.22 | convolution fusion | flops 1610612736 | bytes 8126464 | tf_op jit(solution)/shard_map/cabf,bfh->cah/dot_general | solution.py:114
  253.3 4.7 %fusion.21 = bf16[64,8,384,1]{2,0,1,3:T(8,128)(2,1)S(1)} fusion(bf16[64,8,4,1024]{3,0,2,1:T(8,128)(2,1)} %bitcast.38, bf16[4,1024,384,1]{2,1,0,3:T(8,128)(2,1)S(1)} %bitcast.180, f32[64,8,384]{2,0,1:T(8,128)S(1)} %convolution_bitcast_fusion.1), kind=kOutput, calls=%fused_computation.30 | convolution fusion | flops 1611792384 | bytes 8519680 | tf_op jit(solution)/shard_map/cabf,bfh->cah/dot_general | solution.py:117
  261.1 4.3 copy.119
  265.4 77.1 %all-to-all-done.2 = bf16[64,32,1024]{2,0,1:T(8,128)(2,1)} async-done(((bf16[64,32,1024]{2,0,1:T(8,128)(2,1)}), bf16[64,32,1024]{2,0,1:T(8,128)(2,1)}, u32[]{:S(2)}, u32[]{:S(2)}) %all-to-all-start.2) | async-done | bytes 4194336 | tf_op jit(solution)/shard_map/all_to_all | solution.py:123
  342.5 4.0 all-to-all-start.4
  355.6 5.3 %convolution_bitcast_fusion.5 = f32[64,1024]{1,0:T(8,128)} fusion(f32[64,32,64]{0,2,1:T(8,128)S(1)} %bitcast.165, bf16[64,32,1024]{2,0,1:T(8,128)(2,1)} %all-to-all-done.2), kind=kOutput, calls=%fused_computation.33 | convolution fusion | flops 1610612736 | bytes 4980736 | tf_op jit(solution)/shard_map/cjr,cjf->rf/dot_general | solution.py:125
  360.9 79.5 %all-to-all-done.4 = bf16[64,32,1024]{2,0,1:T(8,128)(2,1)} async-done(((bf16[64,32,1024]{2,0,1:T(8,128)(2,1)}), bf16[64,32,1024]{2,0,1:T(8,128)(2,1)}, u32[]{:S(2)}, u32[]{:S(2)}) %all-to-all-start.4) | async-done | bytes 4194336 | tf_op jit(solution)/shard_map/all_to_all | solution.py:123
  441.6 4.2 convolution_bitcast_fusion.4
  (78 shorter events, 48.5 us)
Async XLA Ops:
  0.0 156.5 %copy-start = (bf16[1,4096,384]{2,1,0:T(8,128)(2,1)S(1)}, bf16[1,4096,384]{2,1,0:T(8,128)(2,1)}, u32[]{:S(2)}) copy-start(bf16[1,4096,384]{2,1,0:T(8,128)(2,1)} %param.25) | copy-start | bytes 9437188
  0.0 8.2 %copy-start.5 = (bf16[32,4,128]{2,1,0:T(4,128)(2,1)S(1)}, bf16[32,4,128]{2,1,0:T(4,128)(2,1)}, u32[]{:S(2)}) copy-start(bf16[32,4,128]{2,1,0:T(4,128)(2,1)} %param.18) | copy-start | bytes 98308
  13.6 8.4 %copy-start.6 = (s32[128,8]{0,1:T(8,128)S(1)}, s32[128,8]{0,1:T(8,128)}, u32[]{:S(2)}) copy-start(s32[128,8]{0,1:T(8,128)} %param.22) | copy-start | bytes 12292
  13.6 11.9 %copy-start.7 = (f32[128,8]{0,1:T(8,128)S(1)}, f32[128,8]{0,1:T(8,128)}, u32[]{:S(2)}) copy-start(f32[128,8]{0,1:T(8,128)} %param.23) | copy-start | bytes 12292
  13.6 11.9 %copy-start.8 = (s32[16]{0:T(128)S(1)}, s32[16]{0:T(128)}, u32[]{:S(2)}) copy-start(s32[16]{0:T(128)} %param.24) | copy-start | bytes 196
  17.8 13.7 %all-to-all-start = ((f32[32,4,1024]{2,0,1:T(8,128)}), f32[32,4,1024]{2,0,1:T(8,128)}, u32[]{:S(2)}, u32[]{:S(2)}) async-start(f32[32,4,1024]{2,0,1:T(8,128)} %copy.99), calls=%async_computation | async-start | bytes 1048576 | tf_op jit(solution)/shard_map/all_to_all | solution.py:68
  39.5 1.4 copy-start.3
  46.4 99.7 %all-to-all-start.1 = ((bf16[64,32,1024]{2,0,1:T(8,128)(2,1)}), bf16[64,32,1024]{2,0,1:T(8,128)(2,1)}, u32[]{:S(2)}, u32[]{:S(2)}) async-start(bf16[64,32,1024]{2,0,1:T(8,128)(2,1)} %copy.106), calls=%async_computation.1 | async-start | bytes 8388608 | tf_op jit(solution)/shard_map/all_to_all | solution.py:111
  146.1 98.2 %all-to-all-start.3 = ((bf16[64,32,1024]{2,0,1:T(8,128)(2,1)}), bf16[64,32,1024]{2,0,1:T(8,128)(2,1)}, u32[]{:S(2)}, u32[]{:S(2)}) async-start(bf16[64,32,1024]{2,0,1:T(8,128)(2,1)} %copy.116), calls=%async_computation.3 | async-start | bytes 8388608 | tf_op jit(solution)/shard_map/all_to_all | solution.py:111
  156.5 4.7 %copy-start.9 = (bf16[1,4096,384]{2,1,0:T(8,128)(2,1)S(1)}, bf16[1,4096,384]{2,1,0:T(8,128)(2,1)}, u32[]{:S(2)}) copy-start(bf16[1,4096,384]{2,1,0:T(8,128)(2,1)} %param.26) | copy-start | bytes 9437188
  161.2 4.7 %copy-start.1 = (bf16[384,4,1024]{2,1,0:T(4,128)(2,1)S(1)}, bf16[384,4,1024]{2,1,0:T(4,128)(2,1)}, u32[]{:S(2)}) copy-start(bf16[384,4,1024]{2,1,0:T(4,128)(2,1)} %reshape_squeeze.11) | copy-start | bytes 9437188
  244.3 98.2 %all-to-all-start.2 = ((bf16[64,32,1024]{2,0,1:T(8,128)(2,1)}), bf16[64,32,1024]{2,0,1:T(8,128)(2,1)}, u32[]{:S(2)}, u32[]{:S(2)}) async-start(bf16[64,32,1024]{2,0,1:T(8,128)(2,1)} %bitcast.164), calls=%async_computation.2 | async-start | bytes 8388608 | tf_op jit(solution)/shard_map/all_to_all | solution.py:123
  248.6 4.7 %copy-start.10 = (bf16[1,4096,384]{2,1,0:T(8,128)(2,1)S(1)}, bf16[1,4096,384]{2,1,0:T(8,128)(2,1)}, u32[]{:S(2)}) copy-start(bf16[1,4096,384]{2,1,0:T(8,128)(2,1)} %param.26) | copy-start | bytes 9437188
  253.3 4.7 %copy-start.2 = (bf16[384,4,1024]{2,1,0:T(4,128)(2,1)S(1)}, bf16[384,4,1024]{2,1,0:T(4,128)(2,1)}, u32[]{:S(2)}) copy-start(bf16[384,4,1024]{2,1,0:T(4,128)(2,1)} %reshape_squeeze.11) | copy-start | bytes 9437188
  342.5 97.9 %all-to-all-start.4 = ((bf16[64,32,1024]{2,0,1:T(8,128)(2,1)}), bf16[64,32,1024]{2,0,1:T(8,128)(2,1)}, u32[]{:S(2)}, u32[]{:S(2)}) async-start(bf16[64,32,1024]{2,0,1:T(8,128)(2,1)} %bitcast.163), calls=%async_computation.4 | async-start | bytes 8388608 | tf_op jit(solution)/shard_map/all_to_all | solution.py:123
  441.6 4.3 copy-start.4
where the time goes:
time: 456 us; the launch traced here: 447 us
  waiting for transfers between devices  308 us (68%)
  local copies, waits for them, and re-layouts  50.1 us (11%)
  matrix products  46 us (10%)
  starting transfers between devices  22.6 us (5%)
  other arithmetic  12.7 us (3%)
  blocking collectives  6.65 us (1%)
    all_to_all x2, waiting for transfers between devices, on_device(): lax.all_to_all(result, ('ep', 'tp'), split_axis=1, concat_axis=1, tiled=T...  157 us
    all_to_all x2, waiting for transfers between devices, on_device(): lax.all_to_all(outgoing, ('ep', 'tp'), split_axis=1, concat_axis=1, tiled...  150 us
    all_to_all x2, starting transfers between devices, on_device(): lax.all_to_all(outgoing, ('ep', 'tp'), split_axis=1, concat_axis=1, tiled...  10 us
    dot_general x2, matrix products, on_device(): jnp.einsum('cjr,cjf->rf', weighted, returned.astype(jnp.float32), precisi...  9.57 us
    dot_general x2, matrix products, on_device(): jnp.einsum('cabf,bfh->cah', blocks, up_split, preferred_element_type=jnp....  9.42 us
    dot_general x2, matrix products, on_device(): jnp.einsum('cabf,bfh->cah', blocks, gate_split, preferred_element_type=jn...  9.32 us
  transfers between devices with their start and end apart: 5, of which 5 were waited for; matrix products, arithmetic and copies ran while one was open for 17% of the time, Pallas kernels for 0%

commit v1 on v0

--- a/solution.py
+++ b/solution.py
@@ -1,6 +1,10 @@
+import functools
+
 import jax
 import jax.numpy as jnp
 from jax import lax
+from jax.experimental import pallas as pl
+from jax.experimental.pallas import tpu as pltpu
 from jax.sharding import PartitionSpec as P
 
 EPSILON = 1e-06
@@ -48,7 +52,7 @@
     )
 
 
-def on_device(
+def routed_device(
     queries,
     cache_keys,
     cache_values,
@@ -133,6 +137,385 @@
     return (stream.astype(jnp.float32) + mixture).astype(jnp.bfloat16)
 
 
+def flip(value):
+    return 1 - value
+
+
+def layer_kernel(
+    full_width,
+    att_ref,
+    residual_ref,
+    gain_ref,
+    table_ref,
+    gate_ref,
+    up_ref,
+    down_ref,
+    out_ref,
+    att_in,
+    stream_ref,
+    sq_out,
+    sq_in,
+    rows_all,
+    pieces,
+    from_mate,
+    from_b,
+    from_a,
+    from_z,
+    wide_w,
+    down_w,
+    acc_ref,
+    load_sem,
+    att_send,
+    att_recv,
+    sq_send,
+    sq_recv,
+    go_send,
+    z_recv,
+    a_recv,
+    b_recv,
+    mate_recv,
+    back_send,
+    back_mate,
+    back_b,
+    back_a,
+    back_z,
+):
+    ep = lax.axis_index("ep")
+    tp = lax.axis_index("tp")
+    z, y = ep // 2, ep % 2
+    x, c = tp // 2, tp % 2
+    hidden_width = gate_ref.shape[1]
+    width = residual_ref.shape[1]
+    own_rows = att_ref.shape[0]
+
+    loads = [
+        pltpu.make_async_copy(gate_ref, wide_w.at[:, pl.ds(0, hidden_width)], load_sem.at[0]),
+        pltpu.make_async_copy(
+            up_ref, wide_w.at[:, pl.ds(hidden_width, hidden_width)], load_sem.at[1]
+        ),
+        pltpu.make_async_copy(down_ref, down_w, load_sem.at[2]),
+    ]
+    for load in loads:
+        load.start()
+
+    z_of = [z, z + 1 - 2 * (z % 2), z + 2 - 4 * (z // 2), 3 - z]
+    tp_of = [tp, tp + 1 - 2 * c, tp + 2 - 4 * x, 3 - tp]
+    mate = (ep, tp_of[1])
+    step_y = 1 - 2 * y
+    step_x = 2 - 4 * x
+    peer_a = (ep + (1 - c) * step_y, tp + c * step_x)
+    peer_b = (ep + c * step_y, tp + (1 - c) * step_x)
+    peer_z = [None] + [(2 * z_of[k] + y, tp) for k in (1, 2, 3)]
+    own_a = y * (1 - c) + x * c
+    own_b = x * (1 - c) + y * c
+
+    def to(device):
+        return {"ep": device[0], "tp": device[1]}
+
+    barrier = pltpu.get_barrier_semaphore()
+    greeted = [mate, peer_a, peer_b, (ep, tp_of[3])] + peer_z[1:]
+    for device in greeted:
+        pl.semaphore_signal(
+            barrier, inc=1, device_id=to(device), device_id_type=pl.DeviceIdType.MESH
+        )
+    pl.semaphore_wait(barrier, len(greeted))
+
+    sent = []
+
+    def push(source, target, send_sem, recv_sem, device):
+        copy = pltpu.make_async_remote_copy(
+            src_ref=source,
+            dst_ref=target,
+            send_sem=send_sem,
+            recv_sem=recv_sem,
+            device_id=to(device),
+            device_id_type=pl.DeviceIdType.MESH,
+        )
+        copy.start()
+        sent.append(copy)
+
+    def arrived(target, recv_sem, device):
+        pltpu.make_async_remote_copy(
+            src_ref=target,
+            dst_ref=target,
+            send_sem=recv_sem,
+            recv_sem=recv_sem,
+            device_id=to(device),
+            device_id_type=pl.DeviceIdType.MESH,
+        ).wait_recv()
+
+    def columns(index):
+        return pl.ds(pl.multiple_of(index * width, width), width)
+
+    for d in (3, 2, 1):
+        push(
+            att_ref.at[:, columns(tp_of[d])],
+            att_in.at[tp],
+            att_send.at[d],
+            att_recv.at[d],
+            (ep, tp_of[d]),
+        )
+    att_in[tp] = att_ref[:, columns(tp)]
+    for d in (1, 2, 3):
+        arrived(att_in.at[tp_of[d]], att_recv.at[d], (ep, tp_of[d]))
+    stream = (
+        residual_ref[...].astype(jnp.float32) + att_in[...].reshape(4 * own_rows, width)
+    ).astype(jnp.bfloat16)
+    stream_ref[...] = stream
+    stream_f = stream.astype(jnp.float32)
+    row_count = stream.shape[0]
+    own_sq = jnp.sum(stream_f * stream_f, axis=1, keepdims=True)
+    sq_out[...] = jnp.broadcast_to(own_sq, (row_count, 128)).T[0:8, :]
+    for d in (3, 2, 1):
+        push(sq_out, sq_in.at[d - 1], sq_send.at[d], sq_recv.at[d], (ep, tp_of[d]))
+    for d in (1, 2, 3):
+        arrived(sq_in.at[d - 1], sq_recv.at[d], (ep, tp_of[d]))
+    squares = sq_out[...] + sq_in[0] + sq_in[1] + sq_in[2]
+    scaled = lax.rsqrt(squares / full_width + EPSILON)
+    scaled = jnp.concatenate([scaled] * 16, axis=0).T[:, 0:1]
+    normed = (stream_ref[...].astype(jnp.float32) * scaled * gain_ref[tp]).astype(jnp.bfloat16)
+    rows_all[z, y, tp] = normed
+
+    def place(ra, rb):
+        a = own_a if ra == 0 else flip(own_a)
+        b = own_b if rb == 0 else flip(own_b)
+        return a * (1 - c) + b * c, a * c + b * (1 - c)
+
+    def slot(k, ra, rb):
+        y_at, x_at = place(ra, rb)
+        return rows_all.at[z_of[k], y_at, 2 * x_at + c]
+
+    def mate_slot(k, ra, rb):
+        y_at, x_at = place(rb, ra)
+        return rows_all.at[z_of[k], y_at, 2 * x_at + flip(c)]
+
+    def go(block, index, recv_sem, device):
+        push(block, block, go_send.at[index], recv_sem, device)
+
+    def forward(k, ra, rb):
+        block = slot(k, ra, rb)
+        if (ra, rb) == (0, 0):
+            go(block, k * 8, a_recv.at[k], peer_a)
+            go(block, k * 8 + 1, b_recv.at[2 * k], peer_b)
+        if (ra, rb) == (1, 0):
+            go(block, k * 8 + 2, b_recv.at[2 * k + 1], peer_b)
+        role = 2 * ra + rb
+        go(block, k * 8 + 3 + role, mate_recv.at[4 * k + role], mate)
+
+    def take_z(k):
+        arrived(slot(k, 0, 0), z_recv.at[k], peer_z[k])
+        forward(k, 0, 0)
+
+    def take_a(k):
+        arrived(slot(k, 1, 0), a_recv.at[k], peer_a)
+        forward(k, 1, 0)
+
+    def take_b(k, ra):
+        arrived(slot(k, ra, 1), b_recv.at[2 * k + ra], peer_b)
+        forward(k, ra, 1)
+
+    slot_id = (ep * 4 + tp) // 2
+
+    def compute(k):
+        for ra in (0, 1):
+            for rb in (0, 1):
+                arrived(mate_slot(k, ra, rb), mate_recv.at[4 * k + 2 * ra + rb], mate)
+        if k == 0:
+            for load in loads:
+                load.wait()
+        z_at = z_of[k]
+        rows = 2 * row_count
+
+        acc_ref[...] = jnp.zeros_like(acc_ref)
+
+        def add_part(t, carry):
+            acc_ref[...] += jnp.dot(
+                rows_all[z_at, :, t].reshape(rows, width),
+                wide_w[columns(t), :],
+                preferred_element_type=jnp.float32,
+            )
+            return carry
+
+        lax.fori_loop(0, 4, add_part, 0)
+        table = table_ref[z_at]
+        lanes = lax.broadcasted_iota(jnp.int32, table.shape, 1)
+        weight = jnp.sum(jnp.where(lanes == slot_id, table, 0.0), axis=1, keepdims=True)
+        gate = acc_ref[:, 0:hidden_width]
+        up = acc_ref[:, hidden_width : 2 * hidden_width]
+        hidden = (gate / (1.0 + jnp.exp(-gate)) * up * weight).astype(jnp.bfloat16)
+        for t in range(4):
+            part = jnp.dot(
+                hidden,
+                down_w[:, t * width : (t + 1) * width],
+                preferred_element_type=jnp.float32,
+            ).astype(jnp.bfloat16)
+            pieces[t % 2, z_at, :, t // 2] = part.reshape(2, row_count, width)
+        push(pieces.at[flip(c), z_at], from_mate.at[z_at], back_send.at[8 * k], back_mate.at[k], mate)
+
+    def back_1(k):
+        z_at = z_of[k]
+        arrived(from_mate.at[z_at], back_mate.at[k], mate)
+        for rb in (1, 0):
+            for ra in (1, 0):
+                y_at, x_at = place(ra, rb)
+                from_mate[z_at, y_at, x_at] = (
+                    from_mate[z_at, y_at, x_at] + pieces[c, z_at, y_at, x_at]
+                )
+                if rb == 1:
+                    push(
+                        from_mate.at[z_at, y_at, x_at],
+                        from_b.at[k, ra],
+                        back_send.at[8 * k + 1 + ra],
+                        back_b.at[2 * k + ra],
+                        peer_b,
+                    )
+
+    def back_2(k):
+        for ra in (1, 0):
+            arrived(from_b.at[k, ra], back_b.at[2 * k + ra], peer_b)
+            y_at, x_at = place(ra, 0)
+            from_b[k, ra] = from_b[k, ra] + from_mate[z_of[k], y_at, x_at]
+            if ra == 1:
+                push(from_b.at[k, 1], from_a.at[k], back_send.at[8 * k + 3], back_a.at[k], peer_a)
+
+    def back_3(k):
+        arrived(from_a.at[k], back_a.at[k], peer_a)
+        from_a[k] = from_a[k] + from_b[k, 0]
+        if k > 0:
+            push(from_a.at[k], from_z.at[k - 1], back_send.at[8 * k + 4], back_z.at[k], peer_z[k])
+
+    for k in (1, 2, 3):
+        push(slot(0, 0, 0), slot(0, 0, 0), go_send.at[32 + k], z_recv.at[k], peer_z[k])
+    forward(0, 0, 0)
+    take_z(1)
+    take_a(0)
+    take_b(0, 0)
+    take_z(2)
+    take_a(1)
+    take_b(0, 1)
+    take_b(1, 0)
+    compute(0)
+    take_z(3)
+    take_a(2)
+    take_b(1, 1)
+    take_b(2, 0)
+    compute(1)
+    back_1(0)
+    take_a(3)
+    take_b(2, 1)
+    take_b(3, 0)
+    compute(2)
+    back_1(1)
+    back_2(0)
+    take_b(3, 1)
+    compute(3)
+    back_1(2)
+    back_2(1)
+    back_3(0)
+    back_1(3)
+    back_2(2)
+    back_3(1)
+    back_2(3)
+    back_3(2)
+    back_3(3)
+    total = stream_ref[...].astype(jnp.float32) + from_a[0].astype(jnp.float32)
+    for k in (1, 2, 3):
+        arrived(from_z.at[k - 1], back_z.at[k], peer_z[k])
+        total = total + from_z[k - 1].astype(jnp.float32)
+    out_ref[...] = total.astype(jnp.bfloat16)
+    for copy in sent:
+        copy.wait_send()
+
+
+def dense_device(
+    queries,
+    cache_keys,
+    cache_values,
+    new_keys,
+    new_values,
+    lengths,
+    residual,
+    norm_gain,
+    routes,
+    route_weights,
+    expert_slot,
+    gate_halves,
+    up_halves,
+    down_halves,
+):
+    experts = expert_slot.shape[0]
+    row_count, width = residual.shape
+    hidden_width = gate_halves.shape[2]
+    full_width = norm_gain.shape[0]
+    chosen = routes[:, :, None] == jnp.arange(experts, dtype=jnp.int32)
+    by_expert = jnp.sum(jnp.where(chosen, route_weights[:, :, None], 0.0), axis=1)
+    slots = expert_slot[:, None] == jnp.arange(experts, dtype=jnp.int32)[None, :]
+    table = jnp.sum(jnp.where(slots[None], by_expert[:, :, None], 0.0), axis=1)
+    table = lax.all_gather(table, "ep", axis=0, tiled=True).reshape(4, 2 * row_count, experts)
+    own_rows = attend(queries, cache_keys, cache_values, new_keys, new_values, lengths)
+    block = (row_count, width)
+    vmem = pl.BlockSpec(memory_space=pltpu.VMEM)
+    anywhere = pl.BlockSpec(memory_space=pl.ANY)
+    dma = pltpu.SemaphoreType.DMA
+    return pl.pallas_call(
+        functools.partial(layer_kernel, full_width),
+        out_shape=jax.ShapeDtypeStruct(block, jnp.bfloat16),
+        in_specs=[vmem] * 4 + [anywhere] * 3,
+        out_specs=vmem,
+        scratch_shapes=[
+            pltpu.VMEM((4, row_count // 4, width), jnp.float32),
+            pltpu.VMEM(block, jnp.bfloat16),
+            pltpu.VMEM((8, 128), jnp.float32),
+            pltpu.VMEM((3, 8, 128), jnp.float32),
+            pltpu.VMEM((4, 2, 4) + block, jnp.bfloat16),
+            pltpu.VMEM((2, 4, 2, 2) + block, jnp.bfloat16),
+            pltpu.VMEM((4, 2, 2) + block, jnp.bfloat16),
+            pltpu.VMEM((4, 2) + block, jnp.bfloat16),
+            pltpu.VMEM((4,) + block, jnp.bfloat16),
+            pltpu.VMEM((3,) + block, jnp.bfloat16),
+            pltpu.VMEM((full_width, 2 * hidden_width), jnp.bfloat16),
+            pltpu.VMEM((hidden_width, full_width), jnp.bfloat16),
+            pltpu.VMEM((2 * row_count, 2 * hidden_width), jnp.float32),
+            dma((3,)),
+            dma((4,)),
+            dma((4,)),
+            dma((4,)),
+            dma((4,)),
+            dma((36,)),
+            dma((4,)),
+            dma((4,)),
+            dma((8,)),
+            dma((16,)),
+            dma((32,)),
+            dma((4,)),
+            dma((8,)),
+            dma((4,)),
+            dma((4,)),
+        ],
+        compiler_params=pltpu.CompilerParams(
+            collective_id=0, has_side_effects=True, vmem_limit_bytes=58 * 1024 * 1024
+        ),
+    )(
+        own_rows,
+        residual,
+        norm_gain.astype(jnp.float32).reshape(4, 1, width),
+        table,
+        gate_halves[0],
+        up_halves[0],
+        down_halves[0],
+    )
+
+
+def on_device(*args):
+    routes, expert_slot = args[8], args[10]
+    half_rows = routes.shape[0] // 2
+    capacity = min(half_rows, 2 * half_rows * routes.shape[1] // expert_slot.shape[0])
+    grid = (lax.axis_size("ep"), lax.axis_size("tp"))
+    if capacity == half_rows and grid == (8, 4) and routes.shape[0] == 128:
+        return dense_device(*args)
+    return routed_device(*args)
+
+
 def solution(mesh):
     return jax.shard_map(
         on_device,

time: 456 us -> 153 us (0.34); the launches traced: 447 us -> 150 us
  waiting for transfers between devices: 308 us -> 0 us
  Pallas kernels: 0 us -> 106 us
  local copies, waits for them, and re-layouts: 50.1 us -> 5.84 us
  matrix products: 46 us -> 4.03 us
  blocking collectives: 6.65 us -> 32.3 us
  starting transfers between devices: 22.6 us -> 0 us
  other arithmetic: 12.7 us -> 2.11 us
    all_to_all x5 -> x0, waiting for transfers between devices: 308 us -> none  [the longest x2 157 us: on_device(): lax.all_to_all(result, ('ep', 'tp'), split_axis=1, concat_axis=1, tiled=T...]
    pallas_call x0 -> x1, Pallas kernels: none -> 106 us  [dense_device(): pl.pallas_call(functools.partial(layer_kernel, full_width), out_shape=jax...]
    dot_general x10 -> x0, matrix products: 37.8 us -> none  [the longest x2 9.57 us: on_device(): jnp.einsum('cjr,cjf->rf', weighted, returned.astype(jnp.float32), precisi...]
    all_gather x0 -> x1, blocking collectives: none -> 32.3 us  [dense_device(): lax.all_gather(table, 'ep', axis=0, tiled=True)]
    all_to_all x5 -> x0, starting transfers between devices: 22.6 us -> none  [the longest x2 10 us: on_device(): lax.all_to_all(outgoing, ('ep', 'tp'), split_axis=1, concat_axis=1, tiled...]
    convert_element_type x8 -> x0, local copies, waits for them, and re-layouts: 21.4 us -> none  [the longest x2 8.6 us: on_device(): outgoing = jnp.einsum('cjr,rf->cjf', select.astype(jnp.bfloat16), batch_r...]
    reshape x4 -> x0, local copies, waits for them, and re-layouts: 7.88 us -> none  [expert_tables(): weighted.T.reshape(experts, capacity, row_count)]
    psum x1 -> x0, blocking collectives: 6.65 us -> none  [on_device(): squares = lax.psum(jnp.sum(stream_f * stream_f, axis=1), 'tp')]
  transfers between devices with their start and end apart: 5 -> 0, of which waited for: 5 -> 0; matrix products, arithmetic and copies ran while one was open for 17% -> 0% of each run, Pallas kernels for 0% -> 0%
where the time goes in v1:
time: 153 us; the launch traced here: 150 us
  Pallas kernels  106 us (69%)
  blocking collectives  32.3 us (21%)
  local copies, waits for them, and re-layouts  5.84 us (4%)
  matrix products  4.03 us (3%)
  other arithmetic  2.11 us (1%)
    pallas_call x1, Pallas kernels, dense_device(): pl.pallas_call(functools.partial(layer_kernel, full_width), out_shape=jax...  106 us
    all_gather x1, blocking collectives, dense_device(): lax.all_gather(table, 'ep', axis=0, tiled=True)  32.3 us
    unnamed x17, local copies, waits for them, and re-layouts  3.95 us

profile of v1, /device:TPU:0, one launch (start us, length us, event | category | flops | bytes accessed | tf_op | source)
XLA Modules:
  0.0 150.1 jit_solution(6258588820036472184)
XLA Ops:
  0.0 1.1 copy.40
  1.2 0.7 iota_compare_fusion.1
  1.9 0.0 copy-done
  1.9 1.3 fusion.14
  3.2 0.0 copy-done.6
  3.2 0.3 fusion.10
  3.5 0.8 copy.30
  4.4 0.6 fusion.9
  4.9 0.0 copy-done.1
  4.9 0.1 copy.32
  5.0 0.0 copy-start.3
  5.0 0.0 copy-start.4
  5.0 0.0 copy-start.5
  5.0 0.0 copy-start.2
  5.0 2.4 %fusion = f32[32,4,8,128]{3,2,1,0:T(8,128)S(1)} fusion(bf16[32,4,1,128]{3,2,1,0:T(2,128)(2,1)S(1)} %copy.32, bf16[32,4,64,128]{3,2,1,0:T(8,128)(2,1)} %bitcast.37, f32[32,4,8]{2,1,0:T(4,128)S(1)} %fusion.9, f32[32,4,8,1]{3,2,1,0:T(8,128)S(1)} %copy.30, f32[32,4,8,64]{3,2,1,0:T(8,128)S(1)} %get-tuple-element.8, f32[32,4,8]{2,1,0:T(4,128)S(1)} %get-tuple-element.6), kind=kOutput, calls=%fused_computation | convolution fusion | flops 21498880 | bytes 2928640 | tf_op jit(solution)/shard_map/rgqp,rgpd->rgqd/dot_general | solution.py:30
  7.5 1.1 copy.45
  8.6 0.0 copy-done.4
  8.6 0.1 iota_compare_fusion.2
  8.7 0.1 select_reduce_fusion
  8.8 32.3 %all_gather.3 = f32[1024,16]{0,1:T(8,128)S(1)} all-gather(f32[128,16]{0,1:T(8,128)S(1)} %select_reduce_fusion), channel_id=1, replica_groups=mesh['groups'=1,'ep'=8,'tp'=4] {'ep'}, dimensions={0}, use_global_device_ids=true | all-gather | bytes 73728 | tf_op jit(solution)/shard_map/all_gather | solution.py:454
  41.1 1.0 copy.33
  42.1 0.6 reshape.71
  42.7 105.7 %shard_map.136 = bf16[128,1024]{1,0:T(8,128)(2,1)} custom-call(f32[32,4096]{1,0:T(8,128)} %bitcast.28, bf16[128,1024]{1,0:T(8,128)(2,1)} %residual_ref.1, f32[4,1,1024]{2,1,0:T(1,128)} %bitcast.34, f32[4,256,16]{2,1,0:T(8,128)} %bitcast.29, bf16[4096,384]{1,0:T(8,128)(2,1)} %bitcast.25, bf16[4096,384]{1,0:T(8,128)(2,1)} %bitcast.26, bf16[384,4096]{1,0:T(8,128)(2,1)} %bitcast.27), custom_call_target="tpu_custom_call" | custom-call | tf_op jit(solution)/shard_map/pallas_call | solution.py:460
  148.4 1.7 %copy.47 = bf16[128,1024]{1,0:T(8,128)(2,1)} copy(bf16[128,1024]{1,0:T(8,128)(2,1)} %shard_map.136) | data formatting | bytes 524288
  (8 shorter events, 0.1 us)
Async XLA Ops:
  0.0 1.9 %copy-start = (bf16[32,8,32,128]{3,2,1,0:T(8,128)(2,1)S(1)}, bf16[32,8,32,128]{3,2,1,0:T(8,128)(2,1)}, u32[]{:S(2)}) copy-start(bf16[32,8,32,128]{3,2,1,0:T(8,128)(2,1)} %param.15) | copy-start | bytes 6291460
  0.0 3.2 %copy-start.6 = (bf16[32,4,128]{2,1,0:T(4,128)(2,1)S(1)}, bf16[32,4,128]{2,1,0:T(4,128)(2,1)}, u32[]{:S(2)}) copy-start(bf16[32,4,128]{2,1,0:T(4,128)(2,1)} %param.17) | copy-start | bytes 98308
  1.9 3.0 %copy-start.1 = (bf16[32,4,128]{2,1,0:T(4,128)(2,1)S(1)}, bf16[32,4,128]{2,1,0:T(4,128)(2,1)}, u32[]{:S(2)}) copy-start(bf16[32,4,128]{2,1,0:T(4,128)(2,1)} %param.18) | copy-start | bytes 98308
  5.0 3.6 %copy-start.3 = (f32[128,8]{0,1:T(8,128)S(1)}, f32[128,8]{0,1:T(8,128)}, u32[]{:S(2)}) copy-start(f32[128,8]{0,1:T(8,128)} %param.23) | copy-start | bytes 12292
  5.0 3.6 %copy-start.4 = (s32[128,8]{0,1:T(8,128)S(1)}, s32[128,8]{0,1:T(8,128)}, u32[]{:S(2)}) copy-start(s32[128,8]{0,1:T(8,128)} %param.22) | copy-start | bytes 12292
  5.0 3.6 %copy-start.5 = (s32[16]{0:T(128)S(1)}, s32[16]{0:T(128)}, u32[]{:S(2)}) copy-start(s32[16]{0:T(128)} %param.24) | copy-start | bytes 196
  5.0 37.1 %copy-start.2 = (bf16[4096]{0:T(1024)(128)(2,1)S(1)}, bf16[4096]{0:T(1024)(128)(2,1)}, u32[]{:S(2)}) copy-start(bf16[4096]{0:T(1024)(128)(2,1)} %param.21) | copy-start | bytes 24580

commit v2 on v1

--- a/solution.py
+++ b/solution.py
@@ -8,6 +8,7 @@
 from jax.sharding import PartitionSpec as P
 
 EPSILON = 1e-06
+UNROLL = 4
 
 
 def attend(queries, cache_keys, cache_values, new_keys, new_values, lengths):
@@ -143,7 +144,12 @@
 
 def layer_kernel(
     full_width,
-    att_ref,
+    lengths_ref,
+    query_ref,
+    key_ref,
+    value_ref,
+    fresh_key_ref,
+    fresh_value_ref,
     residual_ref,
     gain_ref,
     table_ref,
@@ -151,10 +157,15 @@
     up_ref,
     down_ref,
     out_ref,
+    keys,
+    values,
+    heads_out,
+    att_out,
     att_in,
     stream_ref,
     sq_out,
     sq_in,
+    tables,
     rows_all,
     pieces,
     from_mate,
@@ -169,6 +180,9 @@
     att_recv,
     sq_send,
     sq_recv,
+    table_send,
+    table_z,
+    table_y,
     go_send,
     z_recv,
     a_recv,
@@ -185,17 +199,30 @@
     z, y = ep // 2, ep % 2
     x, c = tp // 2, tp % 2
     hidden_width = gate_ref.shape[1]
-    width = residual_ref.shape[1]
-    own_rows = att_ref.shape[0]
-
+    row_count, width = residual_ref.shape
+    half_rows = row_count // 2
+    own_rows, head_count, head_dim = query_ref.shape
+    own_half = own_rows // 2
+    kv_heads = fresh_key_ref.shape[1]
+    span = key_ref.shape[1] // kv_heads
+    group = head_count // kv_heads
+
+    def half_load(source, target, h, index):
+        part = pl.ds(h * own_half, own_half)
+        return pltpu.make_async_copy(source.at[part], target.at[part], load_sem.at[index])
+
+    cache_loads = [
+        [half_load(key_ref, keys, h, 2 * h), half_load(value_ref, values, h, 2 * h + 1)]
+        for h in (0, 1)
+    ]
     loads = [
-        pltpu.make_async_copy(gate_ref, wide_w.at[:, pl.ds(0, hidden_width)], load_sem.at[0]),
+        pltpu.make_async_copy(gate_ref, wide_w.at[:, pl.ds(0, hidden_width)], load_sem.at[4]),
         pltpu.make_async_copy(
-            up_ref, wide_w.at[:, pl.ds(hidden_width, hidden_width)], load_sem.at[1]
+            up_ref, wide_w.at[:, pl.ds(hidden_width, hidden_width)], load_sem.at[5]
         ),
-        pltpu.make_async_copy(down_ref, down_w, load_sem.at[2]),
+        pltpu.make_async_copy(down_ref, down_w, load_sem.at[6]),
     ]
-    for load in loads:
+    for load in cache_loads[0] + cache_loads[1] + loads:
         load.start()
 
     z_of = [z, z + 1 - 2 * (z % 2), z + 2 - 4 * (z // 2), 3 - z]
@@ -203,6 +230,7 @@
     mate = (ep, tp_of[1])
     step_y = 1 - 2 * y
     step_x = 2 - 4 * x
+    peer_y = (ep + step_y, tp)
     peer_a = (ep + (1 - c) * step_y, tp + c * step_x)
     peer_b = (ep + c * step_y, tp + (1 - c) * step_x)
     peer_z = [None] + [(2 * z_of[k] + y, tp) for k in (1, 2, 3)]
@@ -218,7 +246,6 @@
         pl.semaphore_signal(
             barrier, inc=1, device_id=to(device), device_id_type=pl.DeviceIdType.MESH
         )
-    pl.semaphore_wait(barrier, len(greeted))
 
     sent = []
 
@@ -247,101 +274,187 @@
     def columns(index):
         return pl.ds(pl.multiple_of(index * width, width), width)
 
-    for d in (3, 2, 1):
+    score_scale = 1.0 / float(head_dim) ** 0.5
+    head_at = lax.broadcasted_iota(jnp.int32, (head_count, kv_heads * span), 0)
+    key_at = lax.broadcasted_iota(jnp.int32, (head_count, kv_heads * span), 1)
+    same_group = head_at // group == key_at // span
+    position = jnp.where(same_group, key_at % span, span)
+
+    def per_head(value):
+        return jnp.concatenate(
+            [jnp.broadcast_to(value[g : g + 1], (group, head_dim)) for g in range(kv_heads)], axis=0
+        )
+
+    def attend_row(row, at):
+        query = query_ref[row]
+        scores = lax.dot_general(
+            query, keys[row], (((1,), (1,)), ((), ())), preferred_element_type=jnp.float32
+        )
+        scores = jnp.where(position < lengths_ref[row], scores * score_scale, -1e30)
+        fresh_key = per_head(fresh_key_ref[row].astype(jnp.float32))
+        fresh = (
+            jnp.sum(query.astype(jnp.float32) * fresh_key, axis=1, keepdims=True) * score_scale
+        )
+        top = jnp.maximum(jnp.max(scores, axis=1, keepdims=True), fresh)
+        weights = jnp.exp(scores - top)
+        fresh_weight = jnp.exp(fresh - top)
+        total = jnp.sum(weights, axis=1, keepdims=True) + fresh_weight
+        mixed = jnp.dot(
+            weights.astype(jnp.bfloat16), values[row], preferred_element_type=jnp.float32
+        )
+        mixed = mixed + fresh_weight * per_head(fresh_value_ref[row].astype(jnp.float32))
+        heads_out[at] = mixed / total
+
+    def attend_half(h):
+        for load in cache_loads[h]:
+            load.wait()
+
+        def some_rows(i, carry):
+            for u in range(UNROLL):
+                attend_row(h * own_half + i * UNROLL + u, i * UNROLL + u)
+            return carry
+
+        lax.fori_loop(0, own_half // UNROLL, some_rows, 0)
+        per_part = head_count // 4
+        for t in range(4):
+            part = heads_out[:, t * per_part : (t + 1) * per_part, :]
+            att_out[h, t] = part.reshape(own_half, width).astype(jnp.bfloat16)
+
+    def send_attention(h):
+        for d in (3, 2, 1):
+            push(
+                att_out.at[h, tp_of[d]],
+                att_in.at[h, tp],
+                att_send.at[4 * h + d],
+                att_recv.at[4 * h + d],
+                (ep, tp_of[d]),
+            )
+        att_in[h, tp] = att_out[h, tp]
+
+    def own_squares(h):
+        for d in (1, 2, 3):
+            arrived(att_in.at[h, tp_of[d]], att_recv.at[4 * h + d], (ep, tp_of[d]))
+        residual = jnp.concatenate(
+            [
+                residual_ref[(2 * t + h) * own_half : (2 * t + h + 1) * own_half]
+                for t in range(4)
+            ],
+            axis=0,
+        )
+        attention = att_in[h].reshape(half_rows, width)
+        stream = (residual.astype(jnp.float32) + attention.astype(jnp.float32)).astype(
+            jnp.bfloat16
+        )
+        stream_ref[h] = stream
+        stream_f = stream.astype(jnp.float32)
+        rows_all[z, y, tp, h * half_rows : (h + 1) * half_rows] = (
+            stream_f * gain_ref[tp]
+        ).astype(jnp.bfloat16)
+        return jnp.sum(stream_f * stream_f, axis=1, keepdims=True)
+
+    def push_table(k):
         push(
-            att_ref.at[:, columns(tp_of[d])],
-            att_in.at[tp],
-            att_send.at[d],
-            att_recv.at[d],
-            (ep, tp_of[d]),
-        )
-    att_in[tp] = att_ref[:, columns(tp)]
-    for d in (1, 2, 3):
-        arrived(att_in.at[tp_of[d]], att_recv.at[d], (ep, tp_of[d]))
-    stream = (
-        residual_ref[...].astype(jnp.float32) + att_in[...].reshape(4 * own_rows, width)
-    ).astype(jnp.bfloat16)
-    stream_ref[...] = stream
-    stream_f = stream.astype(jnp.float32)
-    row_count = stream.shape[0]
-    own_sq = jnp.sum(stream_f * stream_f, axis=1, keepdims=True)
-    sq_out[...] = jnp.broadcast_to(own_sq, (row_count, 128)).T[0:8, :]
-    for d in (3, 2, 1):
-        push(sq_out, sq_in.at[d - 1], sq_send.at[d], sq_recv.at[d], (ep, tp_of[d]))
-    for d in (1, 2, 3):
-        arrived(sq_in.at[d - 1], sq_recv.at[d], (ep, tp_of[d]))
-    squares = sq_out[...] + sq_in[0] + sq_in[1] + sq_in[2]
-    scaled = lax.rsqrt(squares / full_width + EPSILON)
-    scaled = jnp.concatenate([scaled] * 16, axis=0).T[:, 0:1]
-    normed = (stream_ref[...].astype(jnp.float32) * scaled * gain_ref[tp]).astype(jnp.bfloat16)
-    rows_all[z, y, tp] = normed
+            tables.at[z_of[k], y],
+            tables.at[z_of[k], y],
+            table_send.at[4 + k],
+            table_y.at[k],
+            peer_y,
+        )
 
     def place(ra, rb):
         a = own_a if ra == 0 else flip(own_a)
         b = own_b if rb == 0 else flip(own_b)
         return a * (1 - c) + b * c, a * c + b * (1 - c)
 
-    def slot(k, ra, rb):
+    def slot(n, ra, rb):
         y_at, x_at = place(ra, rb)
-        return rows_all.at[z_of[k], y_at, 2 * x_at + c]
-
-    def mate_slot(k, ra, rb):
+        return rows_all.at[
+            z_of[n // 2], y_at, 2 * x_at + c, pl.ds(n % 2 * half_rows, half_rows)
+        ]
+
+    def mate_slot(n, ra, rb):
         y_at, x_at = place(rb, ra)
-        return rows_all.at[z_of[k], y_at, 2 * x_at + flip(c)]
+        return rows_all.at[
+            z_of[n // 2], y_at, 2 * x_at + flip(c), pl.ds(n % 2 * half_rows, half_rows)
+        ]
 
     def go(block, index, recv_sem, device):
         push(block, block, go_send.at[index], recv_sem, device)
 
-    def forward(k, ra, rb):
-        block = slot(k, ra, rb)
+    def forward(n, ra, rb):
+        block = slot(n, ra, rb)
         if (ra, rb) == (0, 0):
-            go(block, k * 8, a_recv.at[k], peer_a)
-            go(block, k * 8 + 1, b_recv.at[2 * k], peer_b)
+            go(block, n * 8, a_recv.at[n], peer_a)
+            go(block, n * 8 + 1, b_recv.at[2 * n], peer_b)
         if (ra, rb) == (1, 0):
-            go(block, k * 8 + 2, b_recv.at[2 * k + 1], peer_b)
+            go(block, n * 8 + 2, b_recv.at[2 * n + 1], peer_b)
         role = 2 * ra + rb
-        go(block, k * 8 + 3 + role, mate_recv.at[4 * k + role], mate)
-
-    def take_z(k):
-        arrived(slot(k, 0, 0), z_recv.at[k], peer_z[k])
-        forward(k, 0, 0)
-
-    def take_a(k):
-        arrived(slot(k, 1, 0), a_recv.at[k], peer_a)
-        forward(k, 1, 0)
-
-    def take_b(k, ra):
-        arrived(slot(k, ra, 1), b_recv.at[2 * k + ra], peer_b)
-        forward(k, ra, 1)
+        go(block, n * 8 + 3 + role, mate_recv.at[4 * n + role], mate)
+
+    def begin(h):
+        for k in (1, 2, 3):
+            go(slot(h, 0, 0), 64 + 3 * h + k - 1, z_recv.at[2 * k + h], peer_z[k])
+        forward(h, 0, 0)
+
+    def take_z(n):
+        if n >= 2:
+            arrived(slot(n, 0, 0), z_recv.at[n], peer_z[n // 2])
+            forward(n, 0, 0)
+
+    def take_a(n):
+        arrived(slot(n, 1, 0), a_recv.at[n], peer_a)
+        forward(n, 1, 0)
+
+    def take_b(n, ra):
+        arrived(slot(n, ra, 1), b_recv.at[2 * n + ra], peer_b)
+        forward(n, ra, 1)
 
     slot_id = (ep * 4 + tp) // 2
 
-    def compute(k):
+    def compute(n):
+        k, h = n // 2, n % 2
+        z_at = z_of[k]
         for ra in (0, 1):
             for rb in (0, 1):
-                arrived(mate_slot(k, ra, rb), mate_recv.at[4 * k + 2 * ra + rb], mate)
-        if k == 0:
+                arrived(mate_slot(n, ra, rb), mate_recv.at[4 * n + 2 * ra + rb], mate)
+        if n == 0:
             for load in loads:
                 load.wait()
-        z_at = z_of[k]
-        rows = 2 * row_count
-
+        if h == 0:
+            arrived(tables.at[z_at, flip(y)], table_y.at[k], peer_y)
+        span_rows = pl.ds(h * half_rows, half_rows)
         acc_ref[...] = jnp.zeros_like(acc_ref)
 
         def add_part(t, carry):
             acc_ref[...] += jnp.dot(
-                rows_all[z_at, :, t].reshape(rows, width),
+                rows_all[z_at, :, t, span_rows].reshape(row_count, width),
                 wide_w[columns(t), :],
                 preferred_element_type=jnp.float32,
             )
             return carry
 
         lax.fori_loop(0, 4, add_part, 0)
-        table = table_ref[z_at]
-        lanes = lax.broadcasted_iota(jnp.int32, table.shape, 1)
-        weight = jnp.sum(jnp.where(lanes == slot_id, table, 0.0), axis=1, keepdims=True)
-        gate = acc_ref[:, 0:hidden_width]
-        up = acc_ref[:, hidden_width : 2 * hidden_width]
+        weights = []
+        scales = []
+        for y_at in (0, 1):
+            table = tables[z_at, y_at]
+            lines = lax.broadcasted_iota(jnp.int32, table.shape, 0)
+            line = jnp.sum(jnp.where(lines == slot_id, table, 0.0), axis=0, keepdims=True)
+            weights.append(
+                jnp.broadcast_to(line, (row_count, row_count)).T[
+                    h * half_rows : (h + 1) * half_rows, 0:1
+                ]
+            )
+            line = table[table.shape[0] - 8 : table.shape[0] - 7]
+            scales.append(
+                jnp.broadcast_to(line, (row_count, row_count)).T[
+                    h * half_rows : (h + 1) * half_rows, 0:1
+                ]
+            )
+        weight = jnp.concatenate(weights, axis=0)
+        scale = jnp.concatenate(scales, axis=0)
+        gate = acc_ref[:, 0:hidden_width] * scale
+        up = acc_ref[:, hidden_width : 2 * hidden_width] * scale
         hidden = (gate / (1.0 + jnp.exp(-gate)) * up * weight).astype(jnp.bfloat16)
         for t in range(4):
             part = jnp.dot(
@@ -349,80 +462,111 @@
                 down_w[:, t * width : (t + 1) * width],
                 preferred_element_type=jnp.float32,
             ).astype(jnp.bfloat16)
-            pieces[t % 2, z_at, :, t // 2] = part.reshape(2, row_count, width)
-        push(pieces.at[flip(c), z_at], from_mate.at[z_at], back_send.at[8 * k], back_mate.at[k], mate)
-
-    def back_1(k):
-        z_at = z_of[k]
-        arrived(from_mate.at[z_at], back_mate.at[k], mate)
+            pieces[h, t % 2, z_at, :, t // 2] = part.reshape(2, half_rows, width)
+        push(
+            pieces.at[h, flip(c), z_at],
+            from_mate.at[h, z_at],
+            back_send.at[8 * n],
+            back_mate.at[n],
+            mate,
+        )
+
+    def back_1(n):
+        h, z_at = n % 2, z_of[n // 2]
+        arrived(from_mate.at[h, z_at], back_mate.at[n], mate)
         for rb in (1, 0):
             for ra in (1, 0):
                 y_at, x_at = place(ra, rb)
-                from_mate[z_at, y_at, x_at] = (
-                    from_mate[z_at, y_at, x_at] + pieces[c, z_at, y_at, x_at]
+                from_mate[h, z_at, y_at, x_at] = (
+                    from_mate[h, z_at, y_at, x_at] + pieces[h, c, z_at, y_at, x_at]
                 )
                 if rb == 1:
                     push(
-                        from_mate.at[z_at, y_at, x_at],
-                        from_b.at[k, ra],
-                        back_send.at[8 * k + 1 + ra],
-                        back_b.at[2 * k + ra],
+                        from_mate.at[h, z_at, y_at, x_at],
+                        from_b.at[n, ra],
+                        back_send.at[8 * n + 1 + ra],
+                        back_b.at[2 * n + ra],
                         peer_b,
                     )
 
-    def back_2(k):
+    def back_2(n):
         for ra in (1, 0):
-            arrived(from_b.at[k, ra], back_b.at[2 * k + ra], peer_b)
+            arrived(from_b.at[n, ra], back_b.at[2 * n + ra], peer_b)
             y_at, x_at = place(ra, 0)
-            from_b[k, ra] = from_b[k, ra] + from_mate[z_of[k], y_at, x_at]
+            from_b[n, ra] = from_b[n, ra] + from_mate[n % 2, z_of[n // 2], y_at, x_at]
             if ra == 1:
-                push(from_b.at[k, 1], from_a.at[k], back_send.at[8 * k + 3], back_a.at[k], peer_a)
-
-    def back_3(k):
-        arrived(from_a.at[k], back_a.at[k], peer_a)
-        from_a[k] = from_a[k] + from_b[k, 0]
-        if k > 0:
-            push(from_a.at[k], from_z.at[k - 1], back_send.at[8 * k + 4], back_z.at[k], peer_z[k])
-
-    for k in (1, 2, 3):
-        push(slot(0, 0, 0), slot(0, 0, 0), go_send.at[32 + k], z_recv.at[k], peer_z[k])
-    forward(0, 0, 0)
-    take_z(1)
-    take_a(0)
-    take_b(0, 0)
-    take_z(2)
-    take_a(1)
-    take_b(0, 1)
-    take_b(1, 0)
-    compute(0)
-    take_z(3)
-    take_a(2)
-    take_b(1, 1)
-    take_b(2, 0)
-    compute(1)
-    back_1(0)
-    take_a(3)
-    take_b(2, 1)
-    take_b(3, 0)
-    compute(2)
-    back_1(1)
-    back_2(0)
-    take_b(3, 1)
-    compute(3)
-    back_1(2)
-    back_2(1)
-    back_3(0)
-    back_1(3)
-    back_2(2)
-    back_3(1)
-    back_2(3)
-    back_3(2)
-    back_3(3)
-    total = stream_ref[...].astype(jnp.float32) + from_a[0].astype(jnp.float32)
-    for k in (1, 2, 3):
-        arrived(from_z.at[k - 1], back_z.at[k], peer_z[k])
-        total = total + from_z[k - 1].astype(jnp.float32)
-    out_ref[...] = total.astype(jnp.bfloat16)
+                push(from_b.at[n, 1], from_a.at[n], back_send.at[8 * n + 3], back_a.at[n], peer_a)
+
+    def back_3(n):
+        arrived(from_a.at[n], back_a.at[n], peer_a)
+        from_a[n] = from_a[n] + from_b[n, 0]
+        if n >= 2:
+            push(
+                from_a.at[n], from_z.at[n], back_send.at[8 * n + 4], back_z.at[n], peer_z[n // 2]
+            )
+
+    def finish(h):
+        total = stream_ref[h].astype(jnp.float32) + from_a[h].astype(jnp.float32)
+        for k in (1, 2, 3):
+            n = 2 * k + h
+            arrived(from_z.at[n], back_z.at[n], peer_z[k])
+            total = total + from_z[n].astype(jnp.float32)
+        total = total.astype(jnp.bfloat16)
+        for t in range(4):
+            out_ref[(2 * t + h) * own_half : (2 * t + h + 1) * own_half] = total[
+                t * own_half : (t + 1) * own_half
+            ]
+
+    attend_half(0)
+    pl.semaphore_wait(barrier, len(greeted))
+    send_attention(0)
+    attend_half(1)
+    send_attention(1)
+    squares_0 = own_squares(0)
+    begin(0)
+    squares_1 = own_squares(1)
+    begin(1)
+    own_sq = jnp.concatenate([squares_0, squares_1], axis=0)
+    sq_out[...] = jnp.broadcast_to(own_sq, (row_count, row_count)).T[0:8, :]
+    for d in (3, 2, 1):
+        push(sq_out, sq_in.at[d - 1], sq_send.at[d], sq_recv.at[d], (ep, tp_of[d]))
+
+    def spread_tables():
+        for d in (1, 2, 3):
+            arrived(sq_in.at[d - 1], sq_recv.at[d], (ep, tp_of[d]))
+        squares = sq_out[...] + sq_in[0] + sq_in[1] + sq_in[2]
+        scaled = lax.rsqrt(squares / full_width + EPSILON)
+        tables[z, y] = jnp.concatenate([table_ref[...], scaled], axis=0)
+        for k in (1, 2, 3):
+            push(tables.at[z, y], tables.at[z, y], table_send.at[k], table_z.at[k], peer_z[k])
+        push_table(0)
+
+    def relay_tables():
+        for k in (1, 2, 3):
+            arrived(tables.at[z_of[k], y], table_z.at[k], peer_z[k])
+            push_table(k)
+
+    order = (0, 1, 2, 4, 6, 3, 5, 7)
+
+    def staged(action, step, lag, *more):
+        if 0 <= step - lag < len(order):
+            action(order[step - lag], *more)
+
+    for step in range(1, len(order) + 6):
+        if step == 2:
+            spread_tables()
+        if step == 4:
+            relay_tables()
+        staged(take_z, step, 0)
+        staged(take_a, step, 1)
+        staged(take_b, step, 1, 0)
+        staged(take_b, step, 2, 1)
+        staged(back_1, step, 4)
+        staged(back_2, step, 5)
+        staged(back_3, step, 6)
+        staged(compute, step, 3)
+    for h in (0, 1):
+        finish(h)
     for copy in sent:
         copy.wait_send()
 
@@ -445,58 +589,78 @@
 ):
     experts = expert_slot.shape[0]
     row_count, width = residual.shape
+    half_rows = row_count // 2
     hidden_width = gate_halves.shape[2]
     full_width = norm_gain.shape[0]
+    own_rows, kv_heads, head_dim = new_keys.shape
+    head_count = queries.shape[1] // head_dim
+    keys_per_row = cache_keys.shape[1] * cache_keys.shape[2]
     chosen = routes[:, :, None] == jnp.arange(experts, dtype=jnp.int32)
     by_expert = jnp.sum(jnp.where(chosen, route_weights[:, :, None], 0.0), axis=1)
     slots = expert_slot[:, None] == jnp.arange(experts, dtype=jnp.int32)[None, :]
     table = jnp.sum(jnp.where(slots[None], by_expert[:, :, None], 0.0), axis=1)
-    table = lax.all_gather(table, "ep", axis=0, tiled=True).reshape(4, 2 * row_count, experts)
-    own_rows = attend(queries, cache_keys, cache_values, new_keys, new_values, lengths)
+    table = table.reshape(4, 2, own_rows // 2, experts).transpose(3, 1, 0, 2)
+    table = table.reshape(experts, row_count)
     block = (row_count, width)
+    half = (half_rows, width)
+    cache = (own_rows, keys_per_row, head_dim)
     vmem = pl.BlockSpec(memory_space=pltpu.VMEM)
+    smem = pl.BlockSpec(memory_space=pltpu.SMEM)
     anywhere = pl.BlockSpec(memory_space=pl.ANY)
     dma = pltpu.SemaphoreType.DMA
     return pl.pallas_call(
         functools.partial(layer_kernel, full_width),
         out_shape=jax.ShapeDtypeStruct(block, jnp.bfloat16),
-        in_specs=[vmem] * 4 + [anywhere] * 3,
+        in_specs=[smem, vmem, anywhere, anywhere] + [vmem] * 5 + [anywhere] * 3,
         out_specs=vmem,
         scratch_shapes=[
-            pltpu.VMEM((4, row_count // 4, width), jnp.float32),
-            pltpu.VMEM(block, jnp.bfloat16),
-            pltpu.VMEM((8, 128), jnp.float32),
-            pltpu.VMEM((3, 8, 128), jnp.float32),
+            pltpu.VMEM(cache, jnp.bfloat16),
+            pltpu.VMEM(cache, jnp.bfloat16),
+            pltpu.VMEM((own_rows // 2, head_count, head_dim), jnp.float32),
+            pltpu.VMEM((2, 4, own_rows // 2, width), jnp.bfloat16),
+            pltpu.VMEM((2, 4, own_rows // 2, width), jnp.bfloat16),
+            pltpu.VMEM((2,) + half, jnp.bfloat16),
+            pltpu.VMEM((8, row_count), jnp.float32),
+            pltpu.VMEM((3, 8, row_count), jnp.float32),
+            pltpu.VMEM((4, 2, experts + 8, row_count), jnp.float32),
             pltpu.VMEM((4, 2, 4) + block, jnp.bfloat16),
-            pltpu.VMEM((2, 4, 2, 2) + block, jnp.bfloat16),
-            pltpu.VMEM((4, 2, 2) + block, jnp.bfloat16),
-            pltpu.VMEM((4, 2) + block, jnp.bfloat16),
-            pltpu.VMEM((4,) + block, jnp.bfloat16),
-            pltpu.VMEM((3,) + block, jnp.bfloat16),
+            pltpu.VMEM((2, 2, 4, 2, 2) + half, jnp.bfloat16),
+            pltpu.VMEM((2, 4, 2, 2) + half, jnp.bfloat16),
+            pltpu.VMEM((8, 2) + half, jnp.bfloat16),
+            pltpu.VMEM((8,) + half, jnp.bfloat16),
+            pltpu.VMEM((8,) + half, jnp.bfloat16),
             pltpu.VMEM((full_width, 2 * hidden_width), jnp.bfloat16),
             pltpu.VMEM((hidden_width, full_width), jnp.bfloat16),
-            pltpu.VMEM((2 * row_count, 2 * hidden_width), jnp.float32),
-            dma((3,)),
+            pltpu.VMEM((row_count, 2 * hidden_width), jnp.float32),
+            dma((7,)),
+            dma((8,)),
+            dma((8,)),
             dma((4,)),
-            dma((4,)),
-            dma((4,)),
-            dma((4,)),
-            dma((36,)),
-            dma((4,)),
-            dma((4,)),
-            dma((8,)),
-            dma((16,)),
-            dma((32,)),
             dma((4,)),
             dma((8,)),
             dma((4,)),
             dma((4,)),
+            dma((72,)),
+            dma((8,)),
+            dma((8,)),
+            dma((16,)),
+            dma((32,)),
+            dma((64,)),
+            dma((8,)),
+            dma((16,)),
+            dma((8,)),
+            dma((8,)),
         ],
         compiler_params=pltpu.CompilerParams(
             collective_id=0, has_side_effects=True, vmem_limit_bytes=58 * 1024 * 1024
         ),
     )(
-        own_rows,
+        lengths,
+        queries.reshape(own_rows, head_count, head_dim),
+        cache_keys.reshape(cache),
+        cache_values.reshape(cache),
+        new_keys,
+        new_values,
         residual,
         norm_gain.astype(jnp.float32).reshape(4, 1, width),
         table,

time: 153 us -> 116 us (0.76); the launches traced: 150 us -> 116 us
  blocking collectives: 32.3 us -> 0 us
  matrix products: 4.03 us -> 0 us
  Pallas kernels: 106 us -> 109 us
  local copies, waits for them, and re-layouts: 5.84 us -> 4.21 us
    all_gather x1 -> x0, blocking collectives: 32.3 us -> none  [dense_device(): lax.all_gather(table, 'ep', axis=0, tiled=True)]
    dot_general x3 -> x0, matrix products: 4.03 us -> none  [the longest x1 2.42 us: attend(): output = jnp.einsum('rgqp,rgpd->rgqd', weights, every_value)]
    pallas_call x1, Pallas kernels: 106 us -> 109 us  [dense_device(): pl.pallas_call(functools.partial(layer_kernel, full_width), out_shape=jax...]
    unnamed x17 -> x2, local copies, waits for them, and re-layouts: 3.95 us -> 3.37 us
where the time goes in v2:
time: 116 us
  Pallas kernels  109 us (94%)
  local copies, waits for them, and re-layouts  4.21 us (4%)
  other arithmetic  2.85 us (2%)
    pallas_call x1, Pallas kernels, dense_device(): pl.pallas_call(functools.partial(layer_kernel, full_width), out_shape=jax...  109 us
    unnamed x2, local copies, waits for them, and re-layouts  3.37 us

profile of v2, /device:TPU:0, one launch (start us, length us, event | category | flops | bytes accessed | tf_op | source)
XLA Modules:
  0.0 115.8 jit_solution(18061405783881280325)
XLA Ops:
  0.0 0.7 iota_compare_fusion.1
  0.7 0.7 select_reduce_fusion.1
  1.4 0.1 select_reduce_fusion
  1.6 1.3 %reshape.48 = f32[4096]{0:T(1024)} convert(bf16[4096]{0:T(1024)(128)(2,1)} %param.21) | non-fusion elementwise | flops 4096 | bytes 24576 | tf_op jit(solution)/shard_map/reshape | solution.py:665
  2.9 0.1 reshape.46
  3.0 0.7 reshape.47.table_ref
  3.7 1.7 %copy.21 = bf16[4,8,32,128]{3,2,1,0:T(8,128)(2,1)} copy(bf16[4,8,32,128]{3,1,2,0:T(8,128)(2,1)} %bitcast.17) | data formatting | bytes 524288
  5.4 108.7 %shard_map.136 = bf16[128,1024]{1,0:T(8,128)(2,1)} custom-call(s32[32]{0:T(128)} %lengths_ref.1, bf16[32,32,128]{2,1,0:T(8,128)(2,1)} %bitcast.16, bf16[32,256,128]{2,1,0:T(8,128)(2,1)} %bitcast.14, bf16[32,256,128]{2,1,0:T(8,128)(2,1)} %bitcast.15, bf16[32,4,128]{2,1,0:T(4,128)(2,1)} %fresh_key_ref.1, bf16[32,4,128]{2,1,0:T(4,128)(2,1)} %fresh_value_ref.1, ...), custom_call_target="tpu_custom_call" | custom-call | tf_op jit(solution)/shard_map/pallas_call | solution.py:611
  114.1 1.7 %copy.23 = bf16[128,1024]{1,0:T(8,128)(2,1)} copy(bf16[128,1024]{1,0:T(8,128)(2,1)} %shard_map.136) | data formatting | bytes 524288
  (1 shorter events, 0.0 us)

commit v3 on v2

--- a/solution.py
+++ b/solution.py
@@ -8,7 +8,7 @@
 from jax.sharding import PartitionSpec as P
 
 EPSILON = 1e-06
-UNROLL = 4
+UNROLL = 8
 
 
 def attend(queries, cache_keys, cache_values, new_keys, new_values, lengths):
@@ -159,6 +159,7 @@
     out_ref,
     keys,
     values,
+    heads_in,
     heads_out,
     att_out,
     att_in,
@@ -201,7 +202,9 @@
     hidden_width = gate_ref.shape[1]
     row_count, width = residual_ref.shape
     half_rows = row_count // 2
-    own_rows, head_count, head_dim = query_ref.shape
+    own_rows = query_ref.shape[0]
+    head_dim = fresh_key_ref.shape[2]
+    head_count = query_ref.shape[1] // head_dim
     own_half = own_rows // 2
     kv_heads = fresh_key_ref.shape[1]
     span = key_ref.shape[1] // kv_heads
@@ -286,7 +289,7 @@
         )
 
     def attend_row(row, at):
-        query = query_ref[row]
+        query = heads_in[at].astype(jnp.bfloat16)
         scores = lax.dot_general(
             query, keys[row], (((1,), (1,)), ((), ())), preferred_element_type=jnp.float32
         )
@@ -314,8 +317,13 @@
                 attend_row(h * own_half + i * UNROLL + u, i * UNROLL + u)
             return carry
 
+        per_part = head_count // 4
+        for t in range(4):
+            part = query_ref[h * own_half : (h + 1) * own_half, t * width : (t + 1) * width]
+            heads_in[:, t * per_part : (t + 1) * per_part, :] = part.astype(jnp.float32).reshape(
+                own_half, per_part, head_dim
+            )
         lax.fori_loop(0, own_half // UNROLL, some_rows, 0)
-        per_part = head_count // 4
         for t in range(4):
             part = heads_out[:, t * per_part : (t + 1) * per_part, :]
             att_out[h, t] = part.reshape(own_half, width).astype(jnp.bfloat16)
@@ -348,7 +356,7 @@
         stream_ref[h] = stream
         stream_f = stream.astype(jnp.float32)
         rows_all[z, y, tp, h * half_rows : (h + 1) * half_rows] = (
-            stream_f * gain_ref[tp]
+            stream_f * gain_ref[:, columns(tp)].astype(jnp.float32)
         ).astype(jnp.bfloat16)
         return jnp.sum(stream_f * stream_f, axis=1, keepdims=True)
 
@@ -617,6 +625,7 @@
             pltpu.VMEM(cache, jnp.bfloat16),
             pltpu.VMEM(cache, jnp.bfloat16),
             pltpu.VMEM((own_rows // 2, head_count, head_dim), jnp.float32),
+            pltpu.VMEM((own_rows // 2, head_count, head_dim), jnp.float32),
             pltpu.VMEM((2, 4, own_rows // 2, width), jnp.bfloat16),
             pltpu.VMEM((2, 4, own_rows // 2, width), jnp.bfloat16),
             pltpu.VMEM((2,) + half, jnp.bfloat16),
@@ -656,13 +665,13 @@
         ),
     )(
         lengths,
-        queries.reshape(own_rows, head_count, head_dim),
+        queries,
         cache_keys.reshape(cache),
         cache_values.reshape(cache),
         new_keys,
         new_values,
         residual,
-        norm_gain.astype(jnp.float32).reshape(4, 1, width),
+        norm_gain.reshape(1, full_width),
         table,
         gate_halves[0],
         up_halves[0],

time: 116 us -> 114 us (0.983)
  other arithmetic: 2.85 us -> 1.55 us
    unnamed x2 -> x1, local copies, waits for them, and re-layouts: 3.37 us -> 1.67 us
    reshape x0 -> x1, local copies, waits for them, and re-layouts: none -> 1.31 us  [dense_device(): norm_gain.reshape(1, full_width)]
    reshape x1 -> x0, other arithmetic: 1.3 us -> none  [dense_device(): norm_gain.astype(jnp.float32).reshape(4, 1, width)]
where the time goes in v3:
time: 114 us
  Pallas kernels  108 us (95%)
  local copies, waits for them, and re-layouts  3.82 us (3%)
  other arithmetic  1.55 us (1%)
    pallas_call x1, Pallas kernels, dense_device(): pl.pallas_call(functools.partial(layer_kernel, full_width), out_shape=jax...  108 us

profile of v3, /device:TPU:0, one launch (start us, length us, event | category | flops | bytes accessed | tf_op | source)
XLA Modules:
  0.0 113.7 jit_solution(506766915604633365)
XLA Ops:
  0.0 0.7 iota_compare_fusion.1
  0.7 0.7 select_reduce_fusion.1
  1.4 0.1 select_reduce_fusion
  1.6 1.3 %reshape.38.gain_ref = bf16[1,4096]{1,0:T(2,128)(2,1)} reshape(bf16[4096]{0:T(1024)(128)(2,1)} %param.21) | data formatting | bytes 16384 | tf_op jit(solution)/shard_map/reshape | solution.py:674
  2.9 0.1 reshape.39
  3.0 0.7 reshape.40.table_ref
  3.7 108.3 %shard_map.136 = bf16[128,1024]{1,0:T(8,128)(2,1)} custom-call(s32[32]{0:T(128)} %lengths_ref.1, bf16[32,4096]{1,0:T(8,128)(2,1)} %query_ref.1, bf16[32,256,128]{2,1,0:T(8,128)(2,1)} %bitcast.11, bf16[32,256,128]{2,1,0:T(8,128)(2,1)} %bitcast.12, bf16[32,4,128]{2,1,0:T(4,128)(2,1)} %fresh_key_ref.1, bf16[32,4,128]{2,1,0:T(4,128)(2,1)} %fresh_value_ref.1, ...), custom_call_target="tpu_custom_call" | custom-call | tf_op jit(solution)/shard_map/pallas_call | solution.py:619
  112.1 1.7 %copy.22 = bf16[128,1024]{1,0:T(8,128)(2,1)} copy(bf16[128,1024]{1,0:T(8,128)(2,1)} %shard_map.136) | data formatting | bytes 524288
  (1 shorter events, 0.0 us)
